TPU v7x, 32 devices: a whole 2x2x4 slice. The times are simulated.
32 devices in a mesh: group: 4 (over y, core), dev: 8 (over z, x).
Axes of the slice: x: 2, y: 2, z: 4, core: 2. Of those that a mesh axis runs over, the one named last changes fastest.
Arguments:
- node_state: bfloat16 [16384, 512], P(('group', 'dev')), may hold values from -6 to 6
- hub_state: bfloat16 [64, 512], P('dev'), may hold values from -6 to 6
- w_edge_in: bfloat16 [512, 256], replicated, may hold values from -0.25 to 0.25
- w_edge_out: bfloat16 [256, 512], replicated, may hold values from -0.375 to 0.375
- w_update: bfloat16 [512, 512], replicated, may hold values from -0.25 to 0.25
- edge_src: int32 [131072], P(('group', 'dev')), may hold values from 0 to 319
- edge_dst: int32 [131072], P(('group', 'dev')), may hold values from 0 to 319
- edge_mask: int32 [131072], P(('group', 'dev')), may hold values 0 or 1
- send_list: int32 [32, 8, 32], P(('group', 'dev')), may hold values from 0 to 511
- send_count: int32 [32, 8], P(('group', 'dev')), may hold values from 8 to 32, as said below
- node_cot: bfloat16 [16384, 512], P(('group', 'dev')), may hold values from -0.059814453 to 0.059814453
- hub_cot: bfloat16 [64, 512], P('dev'), may hold values from -0.059814453 to 0.059814453
Outputs:
- new_state: bfloat16 [16384, 512], P(('group', 'dev'))
- new_hub: bfloat16 [64, 512], P('dev')
- grad_in: float32 [512, 256], replicated
- grad_out: float32 [256, 512], replicated
- grad_update: float32 [512, 512], replicated
Inputs may be any that keep to these rules, and one draw needn't show every extreme that they name: Device 0 sends 32 live slots to peer 0: send_count[0, 0] = 32.
All inputs are finite; a program needn't handle non-finite values. No bound on the sum of `edge_mask` on one device may be relied on, other than what follows from the above.
Results may differ from a plain program's by a relative error of at most 0.0064.
The roundings to bfloat16 on the way count: a program that leaves them out, or rounds other values in their place, can miss the bound.
Values may be sent and summed in bfloat16 or wider, within the bound.
No kernel may reach another device: no remote copies, remote signals or barrier semaphores. Data moves between devices by JAX's collectives and lax.ppermute only.
A program may use at most 64 MiB of HBM per device.

v0:
```python
import jax
import jax.numpy as jnp
from jax import lax
from jax.sharding import PartitionSpec as P


def silu_grad(values):
    sigmoid_v = jax.nn.sigmoid(values)
    return sigmoid_v * (1.0 + values * (1.0 - sigmoid_v))


def finish(states, summed, degree, w_update):
    mean_part = summed / jnp.maximum(degree, 1.0)[:, None]
    mixed_rows = (states.astype(jnp.float32) + mean_part).astype(jnp.bfloat16)
    pre_update = jnp.dot(mixed_rows, w_update, preferred_element_type=jnp.float32)
    updated = (states.astype(jnp.float32) + jax.nn.silu(pre_update)).astype(jnp.bfloat16)
    return (mixed_rows, pre_update, updated)


def backward_rows(cotangent, pre_update, degree, w_update):
    grad_pre = (cotangent.astype(jnp.float32) * silu_grad(pre_update)).astype(jnp.bfloat16)
    grad_mix = jnp.dot(grad_pre, w_update.T, preferred_element_type=jnp.float32)
    grad_sum = (grad_mix / jnp.maximum(degree, 1.0)[:, None]).astype(jnp.bfloat16)
    return (grad_pre, grad_sum)


def shards(
    node_state,
    hub_state,
    w_edge_in,
    w_edge_out,
    w_update,
    edge_src,
    edge_dst,
    edge_mask,
    send_list,
    send_count,
    node_cot,
    hub_cot,
):
    width = node_state.shape[1]
    master_rows = node_state.shape[0]
    send_rows = send_list[0]
    peer_total = send_rows.shape[0]
    slot_width = send_rows.shape[1]
    mirror_total = peer_total * slot_width
    live_slot = jnp.arange(slot_width)[None, :] < send_count[0][:, None]
    flat_rows = send_rows.reshape(-1)
    flat_live = live_slot.reshape(-1)
    selector = (
        (flat_rows[:, None] == jnp.arange(master_rows)[None, :]) & flat_live[:, None]
    ).astype(jnp.bfloat16)
    contract = (((0,), (0,)), ((), ()))
    outgoing = jnp.dot(selector, node_state, preferred_element_type=jnp.float32).astype(
        jnp.bfloat16
    )
    mirror_rows = lax.all_to_all(
        outgoing.reshape(peer_total, slot_width, width),
        "dev",
        split_axis=0,
        concat_axis=0,
        tiled=True,
    )
    hub_table = lax.all_gather(hub_state, "dev", axis=0, tiled=True)
    local_table = jnp.concatenate([mirror_rows.reshape(mirror_total, width), hub_table], axis=0)
    local_rows = local_table.shape[0]
    edge_total = edge_src.shape[0]
    block_size = min(1024, edge_total)
    block_count = edge_total // block_size
    sources = edge_src.reshape(block_count, block_size)
    targets = edge_dst.reshape(block_count, block_size)
    edge_keep = edge_mask.reshape(block_count, block_size)
    row_ids = jnp.arange(local_rows)[None, :]

    def forward_step(totals, pieces):
        source_ids, target_ids, keep_ids = pieces
        gathered = local_table[source_ids]
        pre_act = jnp.dot(gathered, w_edge_in, preferred_element_type=jnp.float32)
        hidden = jax.nn.silu(pre_act).astype(jnp.bfloat16)
        message = jnp.dot(hidden, w_edge_out, preferred_element_type=jnp.float32).astype(
            jnp.bfloat16
        )
        onehot = ((target_ids[:, None] == row_ids) & (keep_ids[:, None] > 0)).astype(jnp.bfloat16)
        added = lax.dot_general(onehot, message, contract, preferred_element_type=jnp.float32)
        tally = jnp.sum(onehot, axis=0, dtype=jnp.float32)
        return ((totals[0] + added, totals[1] + tally), pre_act)

    start_fwd = (jnp.zeros((local_rows, width), jnp.float32), jnp.zeros((local_rows,), jnp.float32))
    (partial_value, counts_local), saved_acts = lax.scan(
        forward_step, start_fwd, (sources, targets, edge_keep)
    )
    mirror_part = (
        partial_value[:mirror_total].reshape(peer_total, slot_width, width).astype(jnp.bfloat16)
    )
    mirror_count = counts_local[:mirror_total].reshape(peer_total, slot_width).astype(jnp.bfloat16)
    back_part, back_count = (
        lax.all_to_all(mirror_part, "dev", split_axis=0, concat_axis=0, tiled=True),
        lax.all_to_all(mirror_count, "dev", split_axis=0, concat_axis=0, tiled=True),
    )
    summed = lax.dot_general(
        selector,
        back_part.reshape(mirror_total, width),
        contract,
        preferred_element_type=jnp.float32,
    )
    degree = lax.dot_general(
        selector, back_count.reshape(mirror_total, 1), contract, preferred_element_type=jnp.float32
    )[:, 0]
    hub_part = partial_value[mirror_total:]
    hub_count = counts_local[mirror_total:]
    whole_part, whole_count = (
        lax.psum(hub_part.astype(jnp.bfloat16), "group").astype(jnp.float32),
        lax.psum(hub_count.astype(jnp.bfloat16), "group").astype(jnp.float32),
    )
    hub_summed, hub_degree = (
        lax.psum_scatter(
            whole_part.astype(jnp.bfloat16), "dev", scatter_dimension=0, tiled=True
        ).astype(jnp.float32),
        lax.psum_scatter(
            whole_count.astype(jnp.bfloat16), "dev", scatter_dimension=0, tiled=True
        ).astype(jnp.float32),
    )
    mixed_rows, pre_update, new_state = finish(node_state, summed, degree, w_update)
    hub_mixed, hub_pre, new_hub = finish(hub_state, hub_summed, hub_degree, w_update)
    grad_pre, grad_sum = backward_rows(node_cot, pre_update, degree, w_update)
    hub_grad_pre, hub_grad_sum = backward_rows(hub_cot, hub_pre, hub_degree, w_update)
    grad_outgoing = jnp.dot(selector, grad_sum, preferred_element_type=jnp.float32).astype(
        jnp.bfloat16
    )
    grad_mirror = lax.all_to_all(
        grad_outgoing.reshape(peer_total, slot_width, width),
        "dev",
        split_axis=0,
        concat_axis=0,
        tiled=True,
    )
    grad_hubs = lax.all_gather(hub_grad_sum, "dev", axis=0, tiled=True)
    grad_table = jnp.concatenate([grad_mirror.reshape(mirror_total, width), grad_hubs], axis=0)
    hub_weight = (lax.axis_index("group") == 0).astype(jnp.float32)
    grad_update = lax.dot_general(
        mixed_rows, grad_pre, contract, preferred_element_type=jnp.float32
    )
    grad_update = grad_update + hub_weight * lax.dot_general(
        hub_mixed, hub_grad_pre, contract, preferred_element_type=jnp.float32
    )

    def backward_step(totals, pieces):
        source_ids, target_ids, keep_ids, pre_act = pieces
        gathered = local_table[source_ids]
        hidden = jax.nn.silu(pre_act).astype(jnp.bfloat16)
        grad_message = jnp.where(
            keep_ids[:, None] > 0, grad_table[target_ids], jnp.zeros((), jnp.bfloat16)
        )
        grad_w_out = lax.dot_general(
            hidden, grad_message, contract, preferred_element_type=jnp.float32
        )
        grad_hidden = jnp.dot(grad_message, w_edge_out.T, preferred_element_type=jnp.float32)
        grad_act = (grad_hidden * silu_grad(pre_act)).astype(jnp.bfloat16)
        grad_w_in = lax.dot_general(
            gathered, grad_act, contract, preferred_element_type=jnp.float32
        )
        return ((totals[0] + grad_w_in, totals[1] + grad_w_out), None)

    start = (jnp.zeros(w_edge_in.shape, jnp.float32), jnp.zeros(w_edge_out.shape, jnp.float32))
    local_grads, _ = lax.scan(backward_step, start, (sources, targets, edge_keep, saved_acts))
    grad_in, grad_out, grad_upd = lax.psum(
        (local_grads[0], local_grads[1], grad_update), ("group", "dev")
    )
    return (new_state, new_hub, grad_in, grad_out, grad_upd)


def solution(mesh):
    return jax.shard_map(
        shards,
        mesh=mesh,
        in_specs=(
            P(("group", "dev"), None),
            P("dev", None),
            P(),
            P(),
            P(),
            P(("group", "dev")),
            P(("group", "dev")),
            P(("group", "dev")),
            P(("group", "dev"), None, None),
            P(("group", "dev"), None),
            P(("group", "dev"), None),
            P("dev", None),
        ),
        out_specs=(P(("group", "dev"), None), P("dev", None), P(), P(), P()),
        check_vma=False,
    )
```

profile of v0, /device:TPU:0, one launch (start us, length us, event | category | flops | bytes accessed | tf_op | source)
XLA Modules:
  0.0 417.0 jit_solution(8544541724577750692)
XLA Ops:
  7.2 0.8 iota_compare_fusion.2
  8.1 0.8 eq.35
  8.8 2.1 convolution_convert_fusion.1
  10.9 7.2 %all-to-all-start = ((bf16[8,32,512]{2,1,0:T(8,128)(2,1)}), bf16[8,32,512]{2,1,0:T(8,128)(2,1)S(1)}, u32[]{:S(2)}, u32[]{:S(2)}) async-start(bf16[8,32,512]{2,1,0:T(8,128)(2,1)} %bitcast.1), calls=%async_computation | async-start | bytes 524288 | tf_op jit(solution)/shard_map/all_to_all | solution.py:57
  18.2 0.7 reshape.192
  18.9 0.7 reshape.193
  19.7 0.7 reshape.194
  20.4 31.2 %all_gather.6 = bf16[64,512]{1,0:T(8,128)(2,1)S(1)} all-gather(bf16[8,512]{1,0:T(8,128)(2,1)} %param.17), channel_id=1, replica_groups=mesh['group'=4,'dev'=8] {'dev'}, dimensions={0}, use_global_device_ids=true | all-gather | bytes 73728 | tf_op jit(solution)/shard_map/all_gather | solution.py:64
  51.7 33.4 %while.28 = (s32[]{:T(128)}, f32[320,512]{1,0:T(8,128)}, f32[320]{0:T(512)S(1)}, f32[4,1024,256]{2,1,0:T(8,128)}, s32[4,1024]{1,0:T(4,128)S(1)}, /*index=5*/s32[...) while((s32[]{:T(128)}, f32[320,512]{1,0:T(8,128)}, ...), condition=%wide.region_2.3_spmd.clone, body=%wide.region_0.2_spmd.clone.sunk | while | flops 876877120 | bytes 10273476 | solution.py:89
  51.8 4.0 gather_fusion
  55.7 1.4 bitcast_dynamic-update-slice_fusion.2
  57.2 1.7 fusion.93
  58.9 0.3 convert_reduce_fusion.2
  59.3 4.0 gather_fusion
  63.3 1.5 bitcast_dynamic-update-slice_fusion.2
  64.8 2.7 fusion.93
  67.5 0.3 convert_reduce_fusion.2
  67.9 4.0 gather_fusion
  71.9 1.4 bitcast_dynamic-update-slice_fusion.2
  73.4 2.7 fusion.93
  76.1 0.3 convert_reduce_fusion.2
  76.5 4.0 gather_fusion
  80.5 1.4 bitcast_dynamic-update-slice_fusion.2
  82.0 2.7 fusion.93
  85.1 0.7 convert_element_type.118
  85.8 5.4 %all-to-all-start.2 = ((bf16[8,1,32]{2,1,0:T(2,128)(2,1)}), bf16[8,1,32]{2,1,0:T(2,128)(2,1)S(1)}, u32[]{:S(2)}, u32[]{:S(2)}) async-start(bf16[8,1,32]{2,1,0:T(2,128)(2,1)} %convert_element_type.118), calls=%async_computation.2 | async-start | bytes 8192 | tf_op jit(solution)/shard_map/all_to_all | solution.py:98
  91.3 0.6 dynamic-slice
  92.5 1.2 convert.8
  93.7 0.7 slice.34
  94.5 0.6 slice.35
  95.1 21.8 %all-reduce = bf16[64]{0:T(256)(128)(2,1)S(1)} all-reduce(bf16[64]{0:T(256)(128)(2,1)S(1)} %slice.27), channel_id=3, replica_groups=mesh['group'=4,'dev'=8] {'dev'}, use_global_device_ids=true, to_apply=%region_6.7.clone | all-reduce | flops 64 | bytes 256
  117.0 3.4 all-to-all-start.1
  120.8 38.2 %reduce-scatter.2.cloned.1.call-done = bf16[8,512]{1,0:T(8,128)(2,1)} async-done(((bf16[64,512]{1,0:T(8,128)(2,1)}), bf16[8,512]{1,0:T(8,128)(2,1)}) %reduce-scatter.2.cloned.1.call-update) | async-done | bytes 8208 | tf_op jit(solution)/shard_map/reduce_scatter | solution.py:116
  159.0 6.0 %all-reduce.2 = (bf16[8,512]{1,0:T(8,128)(2,1)S(1)}, bf16[8]{0:T(256)(128)(2,1)S(1)}) all-reduce(bf16[8,512]{1,0:T(8,128)(2,1)} %reduce-scatter.2.cloned.1.call-done, bf16[8]{0:T(256)(128)(2,1)S(1)} %dynamic-slice.1), channel_id=1, replica_groups=mesh['group'=4,'dev'=8] {'group'}, use_global_device_ids=true, to_apply=%region_3.4 | all-reduce | flops 4104 | bytes 16416 | tf_op jit(solution)/shard_map/psum | solution.py:112
  165.0 0.8 fusion.60
  166.1 30.5 %all_gather.7 = bf16[64,512]{1,0:T(8,128)(2,1)S(1)} all-gather(bf16[8,512]{1,0:T(8,128)(2,1)S(1)} %fusion.42), channel_id=1, replica_groups=mesh['group'=4,'dev'=8] {'dev'}, dimensions={0}, use_global_device_ids=true | all-gather | bytes 73728 | tf_op jit(solution)/shard_map/all_gather | solution.py:137
  196.6 1.5 fusion.38
  198.2 2.7 multiply_convert_fusion.3
  200.9 1.4 fusion.41
  202.3 3.6 all-to-all-start.3
  205.9 0.5 fusion.64
  206.4 1.4 fusion.36
  207.8 6.3 %all-to-all-done.3 = bf16[8,32,512]{2,1,0:T(8,128)(2,1)S(1)} async-done(((bf16[8,32,512]{2,1,0:T(8,128)(2,1)}), bf16[8,32,512]{2,1,0:T(8,128)(2,1)S(1)}, u32[]{:S(2)}, u32[]{:S(2)}) %all-to-all-start.3) | async-done | bytes 262176 | tf_op jit(solution)/shard_map/all_to_all | solution.py:130
  214.1 56.7 %while.29 = (s32[]{:T(128)}, f32[512,256]{1,0:T(8,128)}, f32[256,512]{1,0:T(8,128)}, s32[4,1024]{1,0:T(4,128)S(1)}, bf16[320,512]{1,0:T(8,128)(2,1)S(1)}, /*inde...) while((s32[]{:T(128)}, f32[512,256]{1,0:T(8,128)}, ...), condition=%wide.region_8.9_spmd.clone, body=%wide.region_7.8_spmd.clone.sunk | while | flops 810558464 | bytes 11845768 | solution.py:165
  214.2 4.0 gather_fusion.2
  218.2 4.0 gather_fusion.1
  222.2 3.3 convolution_add_fusion.4
  225.5 2.6 convolution_add_fusion.5
  228.1 4.0 gather_fusion.2
  232.1 4.0 gather_fusion.1
  236.1 3.4 convolution_add_fusion.4
  239.6 2.8 convolution_add_fusion.5
  242.4 4.0 gather_fusion.2
  246.3 4.0 gather_fusion.1
  250.4 3.4 convolution_add_fusion.4
  253.8 2.8 convolution_add_fusion.5
  256.6 4.0 gather_fusion.2
  260.6 4.0 gather_fusion.1
  264.6 3.4 convolution_add_fusion.4
  268.0 2.7 convolution_add_fusion.5
  270.8 133.3 %all-reduce.5.cloned.1.call-done = (f32[512,256]{1,0:T(8,128)}, f32[256,512]{1,0:T(8,128)}, f32[512,512]{1,0:T(8,128)}) async-done(((f32[512,256]{1,0:T(8,128)}, f32[256,512]{1,0:T(8,128)}, f32[512,512]{1,0:T(8,128)}), (f32[512,256]{1,0:T(8,128)}, f32[256,512]{1,0:T(8,128)}, f32[512,512]{1,0:T(8,128)})) %all-reduce.5.cloned.1.call-update) | async-done | bytes 2097168 | tf_op jit(solution)/shard_map/psum | solution.py:166
  404.1 1.9 copy.44
  406.0 1.9 copy.45
  407.9 2.3 copy.46
  (88 shorter events, 1.9 us)
Async XLA Ops:
  7.2 157.8 %copy-start = (bf16[512,512]{1,0:T(8,128)(2,1)S(1)}, bf16[512,512]{1,0:T(8,128)(2,1)}, u32[]{:S(2)}) copy-start(bf16[512,512]{1,0:T(8,128)(2,1)} %param.20) | copy-start | bytes 1572868
  10.9 40.7 %all-to-all-start = ((bf16[8,32,512]{2,1,0:T(8,128)(2,1)}), bf16[8,32,512]{2,1,0:T(8,128)(2,1)S(1)}, u32[]{:S(2)}, u32[]{:S(2)}) async-start(bf16[8,32,512]{2,1,0:T(8,128)(2,1)} %bitcast.1), calls=%async_computation | async-start | bytes 524288 | tf_op jit(solution)/shard_map/all_to_all | solution.py:57
  51.7 39.6 %copy-start.6 = (u32[32]{0:T(128)S(1)}, u32[32]{0:T(128)}, u32[]{:S(2)}) copy-start(u32[32]{0:T(128)} %constant.65) | copy-start | bytes 388
  51.7 113.3 %copy-start.2 = (bf16[8,512]{1,0:T(8,128)(2,1)S(1)}, bf16[8,512]{1,0:T(8,128)(2,1)}, u32[]{:S(2)}) copy-start(bf16[8,512]{1,0:T(8,128)(2,1)} %param.17) | copy-start | bytes 24580
  51.7 114.2 %copy-start.3 = (bf16[8,512]{1,0:T(8,128)(2,1)S(1)}, bf16[8,512]{1,0:T(8,128)(2,1)}, u32[]{:S(2)}) copy-start(bf16[8,512]{1,0:T(8,128)(2,1)} %param.27) | copy-start | bytes 24580
  51.7 4.0 copy-start.1
  51.8 5.5 %copy-start.5 = (bf16[256,512]{1,0:T(8,128)(2,1)S(1)}, bf16[256,512]{1,0:T(8,128)(2,1)}, u32[]{:S(2)}) copy-start(bf16[256,512]{1,0:T(8,128)(2,1)} %get-tuple-element.406) | copy-start | bytes 786436 | tf_op jit(solution)/shard_map/while
  59.2 4.0 copy-start.1
  59.3 5.5 %copy-start.5 = (bf16[256,512]{1,0:T(8,128)(2,1)S(1)}, bf16[256,512]{1,0:T(8,128)(2,1)}, u32[]{:S(2)}) copy-start(bf16[256,512]{1,0:T(8,128)(2,1)} %get-tuple-element.406) | copy-start | bytes 786436 | tf_op jit(solution)/shard_map/while
  67.9 4.0 copy-start.1
  67.9 5.5 %copy-start.5 = (bf16[256,512]{1,0:T(8,128)(2,1)S(1)}, bf16[256,512]{1,0:T(8,128)(2,1)}, u32[]{:S(2)}) copy-start(bf16[256,512]{1,0:T(8,128)(2,1)} %get-tuple-element.406) | copy-start | bytes 786436 | tf_op jit(solution)/shard_map/while
  76.5 4.0 copy-start.1
  76.5 5.5 %copy-start.5 = (bf16[256,512]{1,0:T(8,128)(2,1)S(1)}, bf16[256,512]{1,0:T(8,128)(2,1)}, u32[]{:S(2)}) copy-start(bf16[256,512]{1,0:T(8,128)(2,1)} %get-tuple-element.406) | copy-start | bytes 786436 | tf_op jit(solution)/shard_map/while
  85.8 31.2 %all-to-all-start.2 = ((bf16[8,1,32]{2,1,0:T(2,128)(2,1)}), bf16[8,1,32]{2,1,0:T(2,128)(2,1)S(1)}, u32[]{:S(2)}, u32[]{:S(2)}) async-start(bf16[8,1,32]{2,1,0:T(2,128)(2,1)} %convert_element_type.118), calls=%async_computation.2 | async-start | bytes 8192 | tf_op jit(solution)/shard_map/all_to_all | solution.py:98
  91.2 67.8 %reduce-scatter.2.cloned.1.call-start = ((), (), s32[]{:S(2)}) async-start(), calls=%async_computation.5 | async-start | bytes 73728 | tf_op jit(solution)/shard_map/reduce_scatter | solution.py:116
  92.5 105.6 %copy-start.4 = (bf16[512,512]{1,0:T(8,128)(2,1)S(1)}, bf16[512,512]{1,0:T(8,128)(2,1)}, u32[]{:S(2)}) copy-start(bf16[512,512]{1,0:T(8,128)(2,1)} %param.26) | copy-start | bytes 1572868
  117.0 79.6 %all-to-all-start.1 = ((bf16[8,32,512]{2,1,0:T(8,128)(2,1)}), bf16[8,32,512]{2,1,0:T(8,128)(2,1)S(1)}, u32[]{:S(2)}, u32[]{:S(2)}) async-start(bf16[8,32,512]{2,1,0:T(8,128)(2,1)} %bitcast.3), calls=%async_computation.1 | async-start | bytes 524288 | tf_op jit(solution)/shard_map/all_to_all | solution.py:97
  202.3 11.8 %all-to-all-start.3 = ((bf16[8,32,512]{2,1,0:T(8,128)(2,1)}), bf16[8,32,512]{2,1,0:T(8,128)(2,1)S(1)}, u32[]{:S(2)}, u32[]{:S(2)}) async-start(bf16[8,32,512]{2,1,0:T(8,128)(2,1)} %bitcast.6), calls=%async_computation.3 | async-start | bytes 524288 | tf_op jit(solution)/shard_map/all_to_all | solution.py:130
  205.9 198.3 %all-reduce.5.cloned.1.call-start = ((), (), s32[]{:S(2)}) async-start(), calls=%async_computation.6 | async-start | bytes 4194304 | tf_op jit(solution)/shard_map/psum | solution.py:166
Sparse Core Ops, SparseCore 0:
  96.0 62.9 reduce-scatter.1
  270.9 133.1 all-reduce.4
where the time goes:
time: 418 us; the launch traced here: 417 us
  waiting for transfers between devices  178 us (43%)
  blocking collectives  89.5 us (21%)
  local copies, waits for them, and re-layouts  59.5 us (14%)
  matrix products  51.1 us (12%)
  starting transfers between devices  19.8 us (5%)
  between operations  14.9 us (4%)
    psum x1, waiting for transfers between devices, shards(): lax.psum((local_grads[0], local_grads[1], grad_update), ('group', 'dev'))  133 us
    reduce_scatter x1, waiting for transfers between devices, shards(): lax.psum_scatter(whole_part.astype(jnp.bfloat16), 'dev', scatter_dimensio...  38.2 us
    all_gather x1, blocking collectives, shards(): hub_table = lax.all_gather(hub_state, 'dev', axis=0, tiled=True)  31.2 us
    all_gather x1, blocking collectives, shards(): grad_hubs = lax.all_gather(hub_grad_sum, 'dev', axis=0, tiled=True)  30.5 us
    unnamed x1, blocking collectives  21.8 us
    gather x4, local copies, waits for them, and re-layouts, backward_step(): grad_table[target_ids]  15.9 us
    gather x4, local copies, waits for them, and re-layouts, backward_step(): gathered = local_table[source_ids]  15.9 us
    gather x4, local copies, waits for them, and re-layouts, forward_step(): gathered = local_table[source_ids]  15.9 us
  transfers between devices with their start and end apart: 6, of which 3 were waited for; matrix products, arithmetic and copies ran while one was open for 2% of the time, Pallas kernels for 0%

commit v1 on v0

--- a/solution.py
+++ b/solution.py
@@ -2,6 +2,7 @@
 import jax.numpy as jnp
 from jax import lax
 from jax.sharding import PartitionSpec as P
+from jax.lax import psum
 
 
 def silu_grad(values):
@@ -163,8 +164,8 @@
 
     start = (jnp.zeros(w_edge_in.shape, jnp.float32), jnp.zeros(w_edge_out.shape, jnp.float32))
     local_grads, _ = lax.scan(backward_step, start, (sources, targets, edge_keep, saved_acts))
-    grad_in, grad_out, grad_upd = lax.psum(
-        (local_grads[0], local_grads[1], grad_update), ("group", "dev")
+    grad_in, grad_out, grad_upd = psum(
+        psum((local_grads[0], local_grads[1], grad_update), "dev"), "group"
     )
     return (new_state, new_hub, grad_in, grad_out, grad_upd)
 

time: 418 us -> 440 us (1.053)
  waiting for transfers between devices: 178 us -> 200 us
    psum x1 -> x2, waiting for transfers between devices: 133 us -> 155 us  [the longest x1 102 us: shards(): psum((local_grads[0], local_grads[1], grad_update), 'dev')]
  transfers between devices with their start and end apart: 6 -> 7, of which waited for: 3 -> 4; matrix products, arithmetic and copies ran while one was open for 2% -> 2% of each run, Pallas kernels for 0% -> 0%
where the time goes in v1:
time: 440 us; the launch traced here: 439 us
  waiting for transfers between devices  200 us (45%)
  blocking collectives  89.5 us (20%)
  local copies, waits for them, and re-layouts  59.5 us (14%)
  matrix products  51.1 us (12%)
  starting transfers between devices  19.8 us (4%)
  between operations  14.6 us (3%)
    psum x1, waiting for transfers between devices, shards(): psum((local_grads[0], local_grads[1], grad_update), 'dev')  102 us
    psum x1, waiting for transfers between devices, shards(): psum(psum((local_grads[0], local_grads[1], grad_update), 'dev'), 'group')  53.4 us
    reduce_scatter x1, waiting for transfers between devices, shards(): lax.psum_scatter(whole_part.astype(jnp.bfloat16), 'dev', scatter_dimensio...  38.2 us
    all_gather x1, blocking collectives, shards(): hub_table = lax.all_gather(hub_state, 'dev', axis=0, tiled=True)  31.2 us
    all_gather x1, blocking collectives, shards(): grad_hubs = lax.all_gather(hub_grad_sum, 'dev', axis=0, tiled=True)  30.5 us
    unnamed x1, blocking collectives  21.8 us
    gather x4, local copies, waits for them, and re-layouts, forward_step(): gathered = local_table[source_ids]  15.9 us
    gather x4, local copies, waits for them, and re-layouts, backward_step(): grad_table[target_ids]  15.9 us
  transfers between devices with their start and end apart: 7, of which 4 were waited for; matrix products, arithmetic and copies ran while one was open for 2% of the time, Pallas kernels for 0%

profile of v1, /device:TPU:0, one launch (start us, length us, event | category | flops | bytes accessed | tf_op | source)
XLA Modules:
  0.0 438.7 jit_solution(2264708601854535573)
XLA Ops:
  7.2 0.8 iota_compare_fusion.2
  8.1 0.8 eq.35
  8.8 2.1 convolution_convert_fusion.1
  10.9 7.2 %all-to-all-start = ((bf16[8,32,512]{2,1,0:T(8,128)(2,1)}), bf16[8,32,512]{2,1,0:T(8,128)(2,1)S(1)}, u32[]{:S(2)}, u32[]{:S(2)}) async-start(bf16[8,32,512]{2,1,0:T(8,128)(2,1)} %bitcast.1), calls=%async_computation | async-start | bytes 524288 | tf_op jit(solution)/shard_map/all_to_all | solution.py:58
  18.2 0.7 reshape.192
  18.9 0.7 reshape.193
  19.7 0.7 reshape.194
  20.4 31.2 %all_gather.6 = bf16[64,512]{1,0:T(8,128)(2,1)S(1)} all-gather(bf16[8,512]{1,0:T(8,128)(2,1)} %param.17), channel_id=1, replica_groups=mesh['group'=4,'dev'=8] {'dev'}, dimensions={0}, use_global_device_ids=true | all-gather | bytes 73728 | tf_op jit(solution)/shard_map/all_gather | solution.py:65
  51.7 33.4 %while.28 = (s32[]{:T(128)}, f32[320,512]{1,0:T(8,128)}, f32[320]{0:T(512)S(1)}, f32[4,1024,256]{2,1,0:T(8,128)}, s32[4,1024]{1,0:T(4,128)S(1)}, /*index=5*/s32[...) while((s32[]{:T(128)}, f32[320,512]{1,0:T(8,128)}, ...), condition=%wide.region_2.3_spmd.clone, body=%wide.region_0.2_spmd.clone.sunk | while | flops 876877120 | bytes 10273476 | solution.py:90
  51.8 4.0 gather_fusion
  55.7 1.4 bitcast_dynamic-update-slice_fusion.2
  57.2 1.7 fusion.93
  58.9 0.3 convert_reduce_fusion.2
  59.3 4.0 gather_fusion
  63.2 1.5 bitcast_dynamic-update-slice_fusion.2
  64.8 2.7 fusion.93
  67.5 0.3 convert_reduce_fusion.2
  67.9 4.0 gather_fusion
  71.9 1.4 bitcast_dynamic-update-slice_fusion.2
  73.4 2.7 fusion.93
  76.5 4.0 gather_fusion
  80.5 1.4 bitcast_dynamic-update-slice_fusion.2
  82.0 2.7 fusion.93
  85.1 0.7 convert_element_type.118
  85.7 5.4 %all-to-all-start.2 = ((bf16[8,1,32]{2,1,0:T(2,128)(2,1)}), bf16[8,1,32]{2,1,0:T(2,128)(2,1)S(1)}, u32[]{:S(2)}, u32[]{:S(2)}) async-start(bf16[8,1,32]{2,1,0:T(2,128)(2,1)} %convert_element_type.118), calls=%async_computation.2 | async-start | bytes 8192 | tf_op jit(solution)/shard_map/all_to_all | solution.py:99
  91.2 0.6 dynamic-slice
  92.5 1.2 convert.8
  93.7 0.7 slice.34
  94.4 0.6 slice.35
  95.1 21.8 %all-reduce = bf16[64]{0:T(256)(128)(2,1)S(1)} all-reduce(bf16[64]{0:T(256)(128)(2,1)S(1)} %slice.27), channel_id=3, replica_groups=mesh['group'=4,'dev'=8] {'dev'}, use_global_device_ids=true, to_apply=%region_6.7.clone | all-reduce | flops 64 | bytes 256
  117.0 3.4 all-to-all-start.1
  120.8 38.2 %reduce-scatter.2.cloned.1.call-done = bf16[8,512]{1,0:T(8,128)(2,1)} async-done(((bf16[64,512]{1,0:T(8,128)(2,1)}), bf16[8,512]{1,0:T(8,128)(2,1)}) %reduce-scatter.2.cloned.1.call-update) | async-done | bytes 8208 | tf_op jit(solution)/shard_map/reduce_scatter | solution.py:117
  158.9 6.0 %all-reduce.3 = (bf16[8,512]{1,0:T(8,128)(2,1)S(1)}, bf16[8]{0:T(256)(128)(2,1)S(1)}) all-reduce(bf16[8,512]{1,0:T(8,128)(2,1)} %reduce-scatter.2.cloned.1.call-done, bf16[8]{0:T(256)(128)(2,1)S(1)} %dynamic-slice.1), channel_id=1, replica_groups=mesh['group'=4,'dev'=8] {'group'}, use_global_device_ids=true, to_apply=%region_3.4 | all-reduce | flops 4104 | bytes 16416 | tf_op jit(solution)/shard_map/psum | solution.py:113
  165.0 0.8 fusion.60
  166.0 30.5 %all_gather.7 = bf16[64,512]{1,0:T(8,128)(2,1)S(1)} all-gather(bf16[8,512]{1,0:T(8,128)(2,1)S(1)} %fusion.42), channel_id=1, replica_groups=mesh['group'=4,'dev'=8] {'dev'}, dimensions={0}, use_global_device_ids=true | all-gather | bytes 73728 | tf_op jit(solution)/shard_map/all_gather | solution.py:138
  196.6 1.5 fusion.38
  198.1 2.7 multiply_convert_fusion.3
  200.8 1.4 fusion.41
  202.2 3.6 all-to-all-start.3
  205.9 0.5 fusion.64
  206.3 1.4 fusion.36
  207.7 6.3 %all-to-all-done.3 = bf16[8,32,512]{2,1,0:T(8,128)(2,1)S(1)} async-done(((bf16[8,32,512]{2,1,0:T(8,128)(2,1)}), bf16[8,32,512]{2,1,0:T(8,128)(2,1)S(1)}, u32[]{:S(2)}, u32[]{:S(2)}) %all-to-all-start.3) | async-done | bytes 262176 | tf_op jit(solution)/shard_map/all_to_all | solution.py:131
  214.1 56.7 %while.29 = (s32[]{:T(128)}, f32[512,256]{1,0:T(8,128)}, f32[256,512]{1,0:T(8,128)}, s32[4,1024]{1,0:T(4,128)S(1)}, bf16[320,512]{1,0:T(8,128)(2,1)S(1)}, /*inde...) while((s32[]{:T(128)}, f32[512,256]{1,0:T(8,128)}, ...), condition=%wide.region_8.9_spmd.clone, body=%wide.region_7.8_spmd.clone.sunk | while | flops 810558464 | bytes 11845768 | solution.py:166
  214.1 4.0 gather_fusion.2
  218.1 4.0 gather_fusion.1
  222.1 3.3 convolution_add_fusion.4
  225.4 2.6 convolution_add_fusion.5
  228.1 4.0 gather_fusion.2
  232.1 4.0 gather_fusion.1
  236.1 3.4 convolution_add_fusion.4
  239.5 2.8 convolution_add_fusion.5
  242.3 4.0 gather_fusion.2
  246.3 4.0 gather_fusion.1
  250.3 3.4 convolution_add_fusion.4
  253.8 2.8 convolution_add_fusion.5
  256.5 4.0 gather_fusion.2
  260.5 4.0 gather_fusion.1
  264.5 3.4 convolution_add_fusion.4
  268.0 2.7 convolution_add_fusion.5
  270.8 102.0 %all-reduce.7.cloned.1.call-done = (f32[512,256]{1,0:T(8,128)}, f32[256,512]{1,0:T(8,128)}, f32[512,512]{1,0:T(8,128)}) async-done(((f32[512,256]{1,0:T(8,128)}, f32[256,512]{1,0:T(8,128)}, f32[512,512]{1,0:T(8,128)}), (f32[512,256]{1,0:T(8,128)}, f32[256,512]{1,0:T(8,128)}, f32[512,512]{1,0:T(8,128)})) %all-reduce.7.cloned.1.call-update) | async-done | bytes 2097168 | tf_op jit(solution)/shard_map/psum | solution.py:168
  372.9 53.4 %all-reduce.9.cloned.1.call-done = (f32[512,256]{1,0:T(8,128)}, f32[256,512]{1,0:T(8,128)}, f32[512,512]{1,0:T(8,128)}) async-done(((f32[512,256]{1,0:T(8,128)}, f32[256,512]{1,0:T(8,128)}, f32[512,512]{1,0:T(8,128)}), (f32[512,256]{1,0:T(8,128)}, f32[256,512]{1,0:T(8,128)}, f32[512,512]{1,0:T(8,128)})) %all-reduce.9.cloned.1.call-update) | async-done | bytes 2097168 | tf_op jit(solution)/shard_map/psum | solution.py:167
  426.2 1.9 copy.47
  428.1 1.9 copy.48
  430.0 2.3 copy.49
  (91 shorter events, 2.3 us)
Async XLA Ops:
  7.2 157.8 %copy-start = (bf16[512,512]{1,0:T(8,128)(2,1)S(1)}, bf16[512,512]{1,0:T(8,128)(2,1)}, u32[]{:S(2)}) copy-start(bf16[512,512]{1,0:T(8,128)(2,1)} %param.20) | copy-start | bytes 1572868
  10.9 40.7 %all-to-all-start = ((bf16[8,32,512]{2,1,0:T(8,128)(2,1)}), bf16[8,32,512]{2,1,0:T(8,128)(2,1)S(1)}, u32[]{:S(2)}, u32[]{:S(2)}) async-start(bf16[8,32,512]{2,1,0:T(8,128)(2,1)} %bitcast.1), calls=%async_computation | async-start | bytes 524288 | tf_op jit(solution)/shard_map/all_to_all | solution.py:58
  51.7 39.6 %copy-start.6 = (u32[32]{0:T(128)S(1)}, u32[32]{0:T(128)}, u32[]{:S(2)}) copy-start(u32[32]{0:T(128)} %constant.65) | copy-start | bytes 388
  51.7 113.3 %copy-start.2 = (bf16[8,512]{1,0:T(8,128)(2,1)S(1)}, bf16[8,512]{1,0:T(8,128)(2,1)}, u32[]{:S(2)}) copy-start(bf16[8,512]{1,0:T(8,128)(2,1)} %param.17) | copy-start | bytes 24580
  51.7 114.1 %copy-start.3 = (bf16[8,512]{1,0:T(8,128)(2,1)S(1)}, bf16[8,512]{1,0:T(8,128)(2,1)}, u32[]{:S(2)}) copy-start(bf16[8,512]{1,0:T(8,128)(2,1)} %param.27) | copy-start | bytes 24580
  51.7 4.0 copy-start.1
  51.8 5.4 %copy-start.5 = (bf16[256,512]{1,0:T(8,128)(2,1)S(1)}, bf16[256,512]{1,0:T(8,128)(2,1)}, u32[]{:S(2)}) copy-start(bf16[256,512]{1,0:T(8,128)(2,1)} %get-tuple-element.409) | copy-start | bytes 786436 | tf_op jit(solution)/shard_map/while
  59.2 4.0 copy-start.1
  59.3 5.5 %copy-start.5 = (bf16[256,512]{1,0:T(8,128)(2,1)S(1)}, bf16[256,512]{1,0:T(8,128)(2,1)}, u32[]{:S(2)}) copy-start(bf16[256,512]{1,0:T(8,128)(2,1)} %get-tuple-element.409) | copy-start | bytes 786436 | tf_op jit(solution)/shard_map/while
  67.9 4.0 copy-start.1
  67.9 5.5 %copy-start.5 = (bf16[256,512]{1,0:T(8,128)(2,1)S(1)}, bf16[256,512]{1,0:T(8,128)(2,1)}, u32[]{:S(2)}) copy-start(bf16[256,512]{1,0:T(8,128)(2,1)} %get-tuple-element.409) | copy-start | bytes 786436 | tf_op jit(solution)/shard_map/while
  76.5 4.0 copy-start.1
  76.5 5.5 %copy-start.5 = (bf16[256,512]{1,0:T(8,128)(2,1)S(1)}, bf16[256,512]{1,0:T(8,128)(2,1)}, u32[]{:S(2)}) copy-start(bf16[256,512]{1,0:T(8,128)(2,1)} %get-tuple-element.409) | copy-start | bytes 786436 | tf_op jit(solution)/shard_map/while
  85.7 31.2 %all-to-all-start.2 = ((bf16[8,1,32]{2,1,0:T(2,128)(2,1)}), bf16[8,1,32]{2,1,0:T(2,128)(2,1)S(1)}, u32[]{:S(2)}, u32[]{:S(2)}) async-start(bf16[8,1,32]{2,1,0:T(2,128)(2,1)} %convert_element_type.118), calls=%async_computation.2 | async-start | bytes 8192 | tf_op jit(solution)/shard_map/all_to_all | solution.py:99
  91.2 67.8 %reduce-scatter.2.cloned.1.call-start = ((), (), s32[]{:S(2)}) async-start(), calls=%async_computation.5 | async-start | bytes 73728 | tf_op jit(solution)/shard_map/reduce_scatter | solution.py:117
  92.5 105.6 %copy-start.4 = (bf16[512,512]{1,0:T(8,128)(2,1)S(1)}, bf16[512,512]{1,0:T(8,128)(2,1)}, u32[]{:S(2)}) copy-start(bf16[512,512]{1,0:T(8,128)(2,1)} %param.26) | copy-start | bytes 1572868
  117.0 79.6 %all-to-all-start.1 = ((bf16[8,32,512]{2,1,0:T(8,128)(2,1)}), bf16[8,32,512]{2,1,0:T(8,128)(2,1)S(1)}, u32[]{:S(2)}, u32[]{:S(2)}) async-start(bf16[8,32,512]{2,1,0:T(8,128)(2,1)} %bitcast.3), calls=%async_computation.1 | async-start | bytes 524288 | tf_op jit(solution)/shard_map/all_to_all | solution.py:98
  202.2 11.8 %all-to-all-start.3 = ((bf16[8,32,512]{2,1,0:T(8,128)(2,1)}), bf16[8,32,512]{2,1,0:T(8,128)(2,1)S(1)}, u32[]{:S(2)}, u32[]{:S(2)}) async-start(bf16[8,32,512]{2,1,0:T(8,128)(2,1)} %bitcast.6), calls=%async_computation.3 | async-start | bytes 524288 | tf_op jit(solution)/shard_map/all_to_all | solution.py:131
  205.8 167.0 %all-reduce.7.cloned.1.call-start = ((), (), s32[]{:S(2)}) async-start(), calls=%async_computation.6 | async-start | bytes 4194304 | tf_op jit(solution)/shard_map/psum | solution.py:168
  270.8 155.5 %all-reduce.9.cloned.1.call-start = ((), (), s32[]{:S(2)}) async-start(), calls=%async_computation.7 | async-start | bytes 4194304 | tf_op jit(solution)/shard_map/psum | solution.py:167
Sparse Core Ops, SparseCore 0:
  96.0 62.9 reduce-scatter.1
  270.9 101.9 all-reduce.6
  375.4 50.8 all-reduce.8
